TPU v7x, 32 devices: a whole 2x2x4 slice. The times are simulated.
32 devices in a mesh: pair: 2 (over x), grow: 4 (over y, core), gcol: 4 (over z).
Axes of the slice: x: 2, y: 2, z: 4, core: 2. Of those that a mesh axis runs over, the one named last changes fastest.
Arguments:
- pair_elements: bfloat16 [1792, 8192], P('pair', ('grow', 'gcol')), may hold values from -0.75 to 0.75
- coulomb_root: float32 [8192], replicated, may hold values from 0.25 to 1
Outputs:
- factored: float32 [8192, 8192], P('grow', ('gcol', 'pair'))
All inputs are finite; a program needn't handle non-finite values.
Results may differ from a plain program's by a relative error of at most 0.0003.
Values may be sent and summed in bfloat16 or wider, within the bound.
A program may use at most 128 MiB of HBM per device.

v0:
```python
import jax
import jax.numpy as jnp
from jax import lax
from jax.sharding import PartitionSpec as P

PANEL = 512
PANELS = 2


def from_root(array, axis, root):
    mine = lax.axis_index(axis) == root
    return lax.psum(jnp.where(mine, array, jnp.zeros_like(array)), axis)


def body(pair_elements, coulomb_root):
    grid_total = coulomb_root.shape[0]
    tile_rows = grid_total // lax.axis_size("grow")
    tile_cols = grid_total // (lax.axis_size("gcol") * lax.axis_size("pair"))
    row_index = lax.axis_index("grow")
    col_index = lax.axis_index("gcol")
    gathered = lax.all_gather(pair_elements, ("grow", "gcol"), axis=1, tiled=True)
    row_block = lax.dynamic_slice_in_dim(gathered, row_index * tile_rows, tile_rows, 1)
    col_block = lax.dynamic_slice_in_dim(gathered, col_index * tile_rows, tile_rows, 1)
    flipped = lax.psum_scatter(
        lax.dot_general(
            col_block, row_block, (((0,), (0,)), ((), ())), preferred_element_type=jnp.float32
        ),
        "pair",
        scatter_dimension=0,
        tiled=True,
    )
    chi_tile = flipped.T
    row_base = row_index * tile_rows
    col_base = lax.axis_index(("gcol", "pair")) * tile_cols
    row_ids = row_base + jnp.arange(tile_rows, dtype=jnp.int32)[:, None]
    col_ids = col_base + jnp.arange(tile_cols, dtype=jnp.int32)[None, :]
    scale_rows = lax.dynamic_slice_in_dim(coulomb_root, row_base, tile_rows, 0)
    scale_cols = lax.dynamic_slice_in_dim(coulomb_root, col_base, tile_cols, 0)
    working = (
        jnp.where(row_ids == col_ids, 1.0, 0.0).astype(jnp.float32)
        + scale_rows[:, None] * chi_tile * scale_cols[None, :]
    )
    packed = jnp.zeros((tile_rows, tile_cols), jnp.float32)
    covered = jnp.zeros((tile_rows, tile_cols), bool)
    owner_width = min(PANEL, tile_cols)
    for step_index in range(PANELS):
        first = step_index * PANEL
        gathered_cols = []
        for owner in range(max(1, PANEL // tile_cols)):
            global_col = first + owner * owner_width
            local_col = global_col % tile_cols
            gathered_cols.append(
                from_root(
                    working[:, local_col : local_col + owner_width],
                    ("gcol", "pair"),
                    global_col // tile_cols,
                )
            )
        panel_cols = jnp.concatenate(gathered_cols, axis=1)
        local_row = first % tile_rows
        diag_block, panel_rows = (
            from_root(panel_cols[local_row : local_row + PANEL], "grow", first // tile_rows),
            from_root(working[local_row : local_row + PANEL], "grow", first // tile_rows),
        )
        factor = jnp.linalg.cholesky(diag_block)
        low_rows = lax.linalg.triangular_solve(
            factor, panel_cols, left_side=False, lower=True, transpose_a=True
        )
        low_cols = lax.linalg.triangular_solve(factor, panel_rows, left_side=True, lower=True)
        working = working - jnp.dot(low_rows, low_cols, precision=lax.Precision.HIGHEST)
        col_pos = col_ids - first
        in_cols = (col_pos >= 0) & (col_pos < PANEL) & (row_ids >= col_ids)
        col_vals = jnp.take(low_rows, jnp.clip(col_pos[0], 0, PANEL - 1), axis=1)
        row_pos = row_ids - first
        in_rows = (row_pos >= 0) & (row_pos < PANEL) & (col_ids > row_ids)
        row_vals = jnp.take(low_cols, jnp.clip(row_pos[:, 0], 0, PANEL - 1), axis=0)
        packed = packed + jnp.where(in_cols, col_vals, 0.0) + jnp.where(in_rows, row_vals, 0.0)
        covered = covered | in_cols | in_rows
    return jnp.where(covered, packed, working)


def solution(mesh):
    return jax.shard_map(
        body,
        mesh=mesh,
        in_specs=(P("pair", ("grow", "gcol")), P()),
        out_specs=P("grow", ("gcol", "pair")),
        check_vma=False,
    )
```

profile of v0, /device:TPU:0, one launch (start us, length us, event | category | flops | bytes accessed | tf_op | source)
XLA Modules:
  0.0 1215.4 jit_solution(15277184497236068876)
XLA Ops:
  7.3 122.0 %all-gather.2.cloned.1.call-done = bf16[896,8192]{1,0:T(8,128)(2,1)} async-done(((bf16[896,512]{1,0:T(8,128)(2,1)}), bf16[896,8192]{1,0:T(8,128)(2,1)}) %all-gather.2.cloned.1.call-update) | async-done | bytes 14680080 | tf_op jit(solution)/shard_map/all_gather | solution.py:21
  129.3 15.1 %fusion.11 = f32[2048,2048]{1,0:T(8,128)} fusion(bf16[896,8192]{1,0:T(8,128)(2,1)} %all-gather.2.cloned.1.call-done, s32[]{:T(128)} %select_n.87, s32[]{:T(128)S(6)} %select_n.88), kind=kOutput, calls=%fused_computation.29 | convolution fusion | flops 7516192768 | bytes 24117764 | tf_op jit(solution)/shard_map/dot_general | solution.py:25
  145.1 186.7 %reduce-scatter.2.cloned.1.call-done = f32[1024,2048]{1,0:T(8,128)} async-done(((f32[2048,2048]{1,0:T(8,128)}), f32[1024,2048]{1,0:T(8,128)}) %reduce-scatter.2.cloned.1.call-update) | async-done | bytes 8388624 | tf_op jit(solution)/shard_map/reduce_scatter | solution.py:24
  345.3 153.2 %all-reduce.8.cloned.1.call-done = f32[2048,512]{0,1:T(8,128)} async-done(((f32[2048,512]{0,1:T(8,128)}), f32[2048,512]{0,1:T(8,128)}) %all-reduce.8.cloned.1.call-update) | async-done | bytes 4194320 | tf_op jit(solution)/shard_map/psum | solution.py:12
  501.4 67.2 %all-reduce.14.cloned.1.call-done = (f32[512,1024]{0,1:T(8,128)}, f32[512,512]{0,1:T(8,128)}) async-done(((f32[512,1024]{0,1:T(8,128)}, f32[512,512]{0,1:T(8,128)}), (f32[512,1024]{0,1:T(8,128)}, f32[512,512]{0,1:T(8,128)})) %all-reduce.14.cloned.1.call-update) | async-done | bytes 3145744 | tf_op jit(solution)/shard_map/psum | solution.py:12
  571.7 11.7 cholesky.286
  583.6 9.8 custom-call.31
  594.1 11.7 cholesky.305
  605.8 10.0 custom-call.32
  616.4 11.7 cholesky.326
  628.2 9.8 custom-call.33
  638.6 11.7 cholesky.343
  663.0 39.3 %custom-call.34 = f32[4,128,128]{1,2,0:T(8,128)S(1)} custom-call(f32[4,128,128]{2,1,0:T(8,128)S(1)} %get-tuple-element.38), custom_call_target="InvertDiagBlocksLowerTriangular" | custom-call | tf_op jit(solution)/shard_map/triangular_solve/custom-call.3 | solution.py:66
  727.0 17.2 %convolution_subtract_fusion = f32[2048,1024]{0,1:T(8,128)S(1)} fusion(f32[2048,1024]{0,1:T(8,128)S(1)} %bitcast.135, f32[128,1024]{1,0:T(8,128)} %fusion.106, f32[128,1024]{1,0:T(8,128)} %copy-done.9, f32[128,1024]{1,0:T(8,128)} %copy-done.7, f32[128,1024]{1,0:T(8,128)} %copy-done.4, f32[2048,128]{0,1:T(8,128)} %fusion.107, f32[2048,128]{0,1:T(8,128)} %copy-done.5, ...), kind=kOutput, calls=%fused_computation.28 | convolution fusion | flops 12891717632 | bytes 23068672 | tf_op jit(solution)/shard_map/dot_general | solution.py:70
  753.1 153.3 %all-reduce.10.cloned.1.call-done = f32[2048,512]{0,1:T(8,128)} async-done(((f32[2048,512]{0,1:T(8,128)}), f32[2048,512]{0,1:T(8,128)}) %all-reduce.10.cloned.1.call-update) | async-done | bytes 4194320 | tf_op jit(solution)/shard_map/psum | solution.py:12
  910.5 9.8 gather_fusion.1
  920.3 9.5 copy.4
  933.3 11.6 gather_fusion
  944.9 31.7 %all-reduce.12.cloned.1.call-done = (f32[512,1024]{0,1:T(8,128)}, f32[512,512]{0,1:T(8,128)}) async-done(((f32[512,1024]{0,1:T(8,128)}, f32[512,512]{0,1:T(8,128)}), (f32[512,1024]{0,1:T(8,128)}, f32[512,512]{0,1:T(8,128)})) %all-reduce.12.cloned.1.call-update) | async-done | bytes 3145744 | tf_op jit(solution)/shard_map/psum | solution.py:12
  979.6 11.7 cholesky.358
  991.5 9.8 custom-call.36
  1002.0 11.7 cholesky.377
  1013.7 10.0 custom-call.37
  1024.4 11.7 cholesky.398
  1036.1 9.8 custom-call.38
  1046.5 11.7 cholesky.415
  1072.3 39.3 %custom-call.39 = f32[4,128,128]{1,2,0:T(8,128)S(1)} custom-call(f32[4,128,128]{2,1,0:T(8,128)S(1)} %get-tuple-element.40), custom_call_target="InvertDiagBlocksLowerTriangular" | custom-call | tf_op jit(solution)/shard_map/triangular_solve/custom-call.3 | solution.py:66
  1122.9 9.8 gather_fusion.3
  1132.7 9.6 copy.7
  1158.4 11.2 gather_fusion.2
  1169.6 29.6 %fusion.8 = f32[2048,1024]{0,1:T(8,128)} fusion(f32[2048,1024]{0,1:T(8,128)} %copy.7, f32[1024,2048]{1,0:T(8,128)} %gather_fusion.2, f32[2048,1024]{0,1:T(8,128)} %copy.4, f32[1024,2048]{1,0:T(8,128)} %gather_fusion, f32[2048,1024]{0,1:T(8,128)} %copy-done.1, s32[2048]{0:T(1024)S(1)} %iota_add_fusion, pred[1024]{0:T(1024)(128)(4,1)S(1)} %get-tuple-element.98, ...), kind=kOutput, calls=%fused_computation.20 | convolution fusion | flops 12935757824 | bytes 56647680 | tf_op jit(solution)/shard_map/dot_general | solution.py:70
  1199.2 9.2 copy.9
  (178 shorter events, 132.9 us)
Async XLA Ops:
  6.5 122.7 %all-gather.2.cloned.1.call-start = ((), (), s32[]{:S(2)}) async-start(), calls=%async_computation.1 | async-start | bytes 15597568 | tf_op jit(solution)/shard_map/all_gather | solution.py:21
  7.3 324.5 %reduce-scatter.2.cloned.1.call-start = ((), (), s32[]{:S(2)}) async-start(), calls=%async_computation.2 | async-start | bytes 25165824 | tf_op jit(solution)/shard_map/reduce_scatter | solution.py:24
  144.3 0.8 copy-start.19
  144.3 187.5 %dynamic-slice-start = ((f32[8192]{0:T(1024)}, s32[]{:T(128)}), f32[2048]{0:T(1024)S(1)}, s32[]{:S(2)}) async-start(f32[8192]{0:T(1024)} %param.12, s32[]{:T(128)} %select_n.87), calls=%async_computation.9 | async-start | bytes 16896 | tf_op jit(solution)/shard_map/dynamic_slice | solution.py:37
  144.4 354.1 %all-reduce.8.cloned.1.call-start = ((), (), s32[]{:S(2)}) async-start(), calls=%async_computation.3 | async-start | bytes 8388608 | tf_op jit(solution)/shard_map/psum | solution.py:12
  336.1 3.4 copy-start
  342.0 226.6 %all-reduce.14.cloned.1.call-start = ((), (), s32[]{:S(2)}) async-start(), calls=%async_computation.6 | async-start | bytes 6291456 | tf_op jit(solution)/shard_map/psum | solution.py:12
  500.8 405.6 %all-reduce.10.cloned.1.call-start = ((), (), s32[]{:S(2)}) async-start(), calls=%async_computation.4 | async-start | bytes 8388608 | tf_op jit(solution)/shard_map/psum | solution.py:12
  663.0 51.9 %copy-start.14 = (f32[512,512]{1,0:T(8,128)}, f32[512,512]{1,0:T(8,128)S(1)}, u32[]{:S(2)}) copy-start(f32[512,512]{1,0:T(8,128)S(1)} %get-tuple-element.218) | copy-start | bytes 3145732
  702.3 4.8 copy-start.17
  704.2 8.2 copy-start.4
  706.4 7.4 copy-start.11
  707.1 7.8 copy-start.7
  709.6 6.4 copy-start.9
  716.0 11.0 slice-start
  717.1 9.9 copy-start.2
  720.0 6.9 slice-start.1
  721.1 3.7 copy-start.5
  744.2 3.4 copy-start.1
  749.9 226.7 %all-reduce.12.cloned.1.call-start = ((), (), s32[]{:S(2)}) async-start(), calls=%async_computation.5 | async-start | bytes 6291456 | tf_op jit(solution)/shard_map/psum | solution.py:12
  920.3 9.5 copy-start.3
  920.3 9.5 copy-start.6
  1072.3 49.1 %copy-start.13 = (f32[512,512]{1,0:T(8,128)}, f32[512,512]{1,0:T(8,128)S(1)}, u32[]{:S(2)}) copy-start(f32[512,512]{1,0:T(8,128)S(1)} %get-tuple-element.217) | copy-start | bytes 3145732
  1111.7 4.5 copy-start.16
  1118.7 3.4 copy-start.12
  1122.1 0.8 copy-start.18
  1142.3 5.9 copy-start.10
  1151.5 6.9 copy-start.8
  1155.9 2.5 copy-start.15
Sparse Core Ops, SparseCore 0:
  9.4 119.7 all-gather.1
  144.5 187.2 reduce-scatter.1
  342.1 156.2 all-reduce.7
  501.0 67.6 all-reduce.13
  750.0 156.3 all-reduce.9
  908.9 67.6 all-reduce.11
where the time goes:
time: 1220 us
  waiting for transfers between devices  715 us (59%)
  other arithmetic  268 us (22%)
  matrix products  114 us (9%)
  local copies, waits for them, and re-layouts  98 us (8%)
  between operations  20 us (2%)
    psum x4, waiting for transfers between devices, from_root(): return lax.psum(jnp.where(mine, array, jnp.zeros_like(array)), axis)  405 us
    reduce_scatter x1, waiting for transfers between devices, body(): lax.psum_scatter(lax.dot_general(col_block, row_block, (((0,), (0,)), (()...  187 us
    another operation x29, other arithmetic, body(): factor = jnp.linalg.cholesky(diag_block)  158 us
    all_gather x1, waiting for transfers between devices, body(): lax.all_gather(pair_elements, ('grow', 'gcol'), axis=1, tiled=True)  122 us
    another operation x7, other arithmetic, body(): lax.linalg.triangular_solve(factor, panel_cols, left_side=False, lower=Tr...  85 us
    dot_general x2, matrix products, body(): jnp.dot(low_rows, low_cols, precision=lax.Precision.HIGHEST)  46.8 us
    gather x4, local copies, waits for them, and re-layouts, body(): row_vals = jnp.take(low_cols, jnp.clip(row_pos[:, 0], 0, PANEL - 1), axis=0)  38.7 us
    another operation x14, matrix products, body(): lax.linalg.triangular_solve(factor, panel_cols, left_side=False, lower=Tr...  26.6 us
  transfers between devices with their start and end apart: 6, of which 6 were waited for; matrix products, arithmetic and copies ran while one was open for 3% of the time, Pallas kernels for 0%

commit v1 on v0

--- a/solution.py
+++ b/solution.py
@@ -9,7 +9,7 @@
 
 def from_root(array, axis, root):
     mine = lax.axis_index(axis) == root
-    return lax.psum(jnp.where(mine, array, jnp.zeros_like(array)), axis)
+    return jnp.sum(lax.all_gather(jnp.where(mine, array, jnp.zeros_like(array)), axis), axis=0)
 
 
 def body(pair_elements, coulomb_root):

time: 1220 us -> 2280 us (1.87)
  waiting for transfers between devices: 715 us -> 1610 us
  local copies, waits for them, and re-layouts: 98 us -> 205 us
  other arithmetic: 268 us -> 322 us
    all_gather x0 -> x6, waiting for transfers between devices: none -> 1300 us  [from_root(): lax.all_gather(jnp.where(mine, array, jnp.zeros_like(array)), axis)]
    psum x4 -> x0, waiting for transfers between devices: 405 us -> none  [from_root(): return lax.psum(jnp.where(mine, array, jnp.zeros_like(array)), axis)]
    unnamed x44 -> x64, local copies, waits for them, and re-layouts: 8.16 us -> 75.4 us
    reduce_sum x0 -> x6, other arithmetic: none -> 54.2 us  [from_root(): jnp.sum(lax.all_gather(jnp.where(mine, array, jnp.zeros_like(array)), axi...]
    all_gather x0 -> x4, local copies, waits for them, and re-layouts: none -> 34.9 us  [from_root(): lax.all_gather(jnp.where(mine, array, jnp.zeros_like(array)), axis)]
  transfers between devices with their start and end apart: 6 -> 8, of which waited for: 6 -> 6; matrix products, arithmetic and copies ran while one was open for 3% -> 8% of each run, Pallas kernels for 0% -> 0%
where the time goes in v1:
time: 2280 us; the launch traced here: 2270 us
  waiting for transfers between devices  1610 us (71%)
  other arithmetic  322 us (14%)
  local copies, waits for them, and re-layouts  205 us (9%)
  matrix products  119 us (5%)
    all_gather x6, waiting for transfers between devices, from_root(): lax.all_gather(jnp.where(mine, array, jnp.zeros_like(array)), axis)  1300 us
    reduce_scatter x1, waiting for transfers between devices, body(): lax.psum_scatter(lax.dot_general(col_block, row_block, (((0,), (0,)), (()...  187 us
    another operation x29, other arithmetic, body(): factor = jnp.linalg.cholesky(diag_block)  159 us
    all_gather x1, waiting for transfers between devices, body(): lax.all_gather(pair_elements, ('grow', 'gcol'), axis=1, tiled=True)  122 us
    another operation x7, other arithmetic, body(): lax.linalg.triangular_solve(factor, panel_cols, left_side=False, lower=Tr...  86.9 us
    unnamed x64, local copies, waits for them, and re-layouts  75.4 us
    reduce_sum x6, other arithmetic, from_root(): jnp.sum(lax.all_gather(jnp.where(mine, array, jnp.zeros_like(array)), axi...  54.2 us
    dot_general x2, matrix products, body(): jnp.dot(low_rows, low_cols, precision=lax.Precision.HIGHEST)  47 us
  transfers between devices with their start and end apart: 8, of which 6 were waited for; matrix products, arithmetic and copies ran while one was open for 8% of the time, Pallas kernels for 0%

profile of v1, /device:TPU:0, one launch (start us, length us, event | category | flops | bytes accessed | tf_op | source)
XLA Modules:
  0.0 2272.6 jit_solution(9183264025690965381)
XLA Ops:
  7.3 122.0 %all-gather.14.cloned.1.call-done = bf16[896,8192]{1,0:T(8,128)(2,1)} async-done(((bf16[896,512]{1,0:T(8,128)(2,1)}), bf16[896,8192]{1,0:T(8,128)(2,1)}) %all-gather.14.cloned.1.call-update) | async-done | bytes 14680080 | tf_op jit(solution)/shard_map/all_gather | solution.py:21
  129.3 15.0 fusion.11
  145.0 186.7 %reduce-scatter.2.cloned.1.call-done = f32[1024,2048]{1,0:T(8,128)} async-done(((f32[2048,2048]{1,0:T(8,128)}), f32[1024,2048]{1,0:T(8,128)}) %reduce-scatter.2.cloned.1.call-update) | async-done | bytes 8388624 | tf_op jit(solution)/shard_map/reduce_scatter | solution.py:24
  345.5 634.4 %all-gather.16.cloned.1.call-done = f32[16384,512]{0,1:T(8,128)} async-done(((f32[2048,512]{0,1:T(8,128)}), f32[16384,512]{0,1:T(8,128)}) %all-gather.16.cloned.1.call-update) | async-done | bytes 33554448 | tf_op jit(solution)/shard_map/all_gather | solution.py:12
  979.9 32.5 %copy.19 = f32[64,8,8,2048]{3,2,1,0:T(8,128)S(1)} copy(f32[64,8,8,2048]{3,1,2,0:T(8,128)} %bitcast.158) | data formatting | bytes 67108864
  1012.4 12.7 bitcast_reduce_fusion.1
  1027.7 11.9 all-gather.20.cloned.1.call-done
  1039.6 11.0 reshape.191
  1060.3 15.3 all-gather.18.cloned.1.call-done
  1088.5 11.7 cholesky.286
  1112.8 11.9 cholesky.305
  1124.8 9.8 custom-call.32
  1136.1 11.7 cholesky.326
  1159.2 12.1 cholesky.343
  1176.9 11.7 while.8
  1188.6 39.3 %custom-call.34 = f32[4,128,128]{1,2,0:T(8,128)S(1)} custom-call(f32[4,128,128]{2,1,0:T(8,128)S(1)} %get-tuple-element.38), custom_call_target="InvertDiagBlocksLowerTriangular" | custom-call | tf_op jit(solution)/shard_map/triangular_solve/custom-call.3 | solution.py:66
  1249.4 17.2 convolution_subtract_fusion
  1275.6 634.6 %all-gather.22.cloned.1.call-done = f32[16384,512]{0,1:T(8,128)} async-done(((f32[2048,512]{0,1:T(8,128)}), f32[16384,512]{0,1:T(8,128)}) %all-gather.22.cloned.1.call-update) | async-done | bytes 33554448 | tf_op jit(solution)/shard_map/all_gather | solution.py:12
  1910.2 32.7 %copy.20 = f32[64,8,8,2048]{3,2,1,0:T(8,128)S(1)} copy(f32[64,8,8,2048]{3,1,2,0:T(8,128)} %bitcast.159) | data formatting | bytes 67108864
  1942.9 12.7 bitcast_reduce_fusion
  1982.4 11.2 gather_fusion
  1993.7 11.3 reshape.194
  2027.1 11.7 cholesky.358
  2051.5 12.1 cholesky.377
  2063.6 9.8 custom-call.37
  2075.0 11.7 cholesky.398
  2098.0 11.9 cholesky.415
  2116.3 12.0 while.9
  2128.3 39.3 %custom-call.39 = f32[4,128,128]{1,2,0:T(8,128)S(1)} custom-call(f32[4,128,128]{2,1,0:T(8,128)S(1)} %get-tuple-element.40), custom_call_target="InvertDiagBlocksLowerTriangular" | custom-call | tf_op jit(solution)/shard_map/triangular_solve/custom-call.3 | solution.py:66
  2182.1 9.9 gather_fusion.3
  2215.0 11.3 gather_fusion.2
  2226.3 29.7 %fusion.8 = f32[2048,1024]{0,1:T(8,128)} fusion(f32[2048,1024]{0,1:T(8,128)} %copy.14, f32[1024,2048]{1,0:T(8,128)} %gather_fusion.2, f32[2048,1024]{0,1:T(8,128)} %copy.11, f32[1024,2048]{1,0:T(8,128)} %gather_fusion, f32[2048,1024]{0,1:T(8,128)} %copy-done.1, s32[2048]{0:T(1024)S(1)} %copy-done.25, pred[1024]{0:T(1024)(128)(4,1)S(1)} %get-tuple-element.94, ...), kind=kOutput, calls=%fused_computation.22 | convolution fusion | flops 12935757824 | bytes 56647680 | tf_op jit(solution)/shard_map/dot_general | solution.py:70
  (214 shorter events, 247.4 us)
Async XLA Ops:
  6.5 122.7 %all-gather.14.cloned.1.call-start = ((), (), s32[]{:S(2)}) async-start(), calls=%async_computation.1 | async-start | bytes 15597568 | tf_op jit(solution)/shard_map/all_gather | solution.py:21
  7.3 324.5 %reduce-scatter.2.cloned.1.call-start = ((), (), s32[]{:S(2)}) async-start(), calls=%async_computation.2 | async-start | bytes 25165824 | tf_op jit(solution)/shard_map/reduce_scatter | solution.py:24
  144.2 187.5 %dynamic-slice-start = ((f32[8192]{0:T(1024)}, s32[]{:T(128)}), f32[2048]{0:T(1024)S(1)}, s32[]{:S(2)}) async-start(f32[8192]{0:T(1024)} %param.12, s32[]{:T(128)} %select_n.87), calls=%async_computation.11 | async-start | bytes 16896 | tf_op jit(solution)/shard_map/dynamic_slice | solution.py:37
  144.3 835.6 %all-gather.16.cloned.1.call-start = ((), (), s32[]{:S(2)}) async-start(), calls=%async_computation.3 | async-start | bytes 37748736 | tf_op jit(solution)/shard_map/all_gather | solution.py:12
  145.0 191.0 %copy-start.27 = (s32[1024]{0:T(1024)}, s32[1024]{0:T(1024)S(1)}, u32[]{:S(2)}) copy-start(s32[1024]{0:T(1024)S(1)} %iota_add_fusion.1) | copy-start | bytes 12292
  145.0 191.0 %copy-start.24 = (s32[2048]{0:T(1024)}, s32[2048]{0:T(1024)S(1)}, u32[]{:S(2)}) copy-start(s32[2048]{0:T(1024)S(1)} %iota_add_fusion) | copy-start | bytes 24580
  342.0 697.7 %all-gather.20.cloned.1.call-start = ((), (), s32[]{:S(2)}) async-start(), calls=%async_computation.5 | async-start | bytes 10485760 | tf_op jit(solution)/shard_map/all_gather | solution.py:12
  345.2 730.5 %all-gather.18.cloned.1.call-start = ((), (), s32[]{:S(2)}) async-start(), calls=%async_computation.4 | async-start | bytes 5242880 | tf_op jit(solution)/shard_map/all_gather | solution.py:12
  1027.4 882.8 %all-gather.22.cloned.1.call-start = ((), (), s32[]{:S(2)}) async-start(), calls=%async_computation.6 | async-start | bytes 37748736 | tf_op jit(solution)/shard_map/all_gather | solution.py:12
  1111.4 118.9 %copy-start.14 = (f32[512,1024]{0,1:T(8,128)S(1)}, f32[512,1024]{0,1:T(8,128)}, u32[]{:S(2)}) copy-start(f32[512,1024]{0,1:T(8,128)} %reduce_sum.56) | copy-start | bytes 6291460
  1228.0 5.6 copy-start.19
  1231.0 7.8 copy-start.6
  1232.9 7.3 copy-start.5
  1233.6 7.8 copy-start.9
  1236.1 6.4 copy-start.13
  1241.4 8.0 slice-start
  1242.5 6.9 copy-start.2
  1244.0 5.4 slice-start.1
  1272.3 721.3 %all-gather.26.cloned.1.call-start = ((), (), s32[]{:S(2)}) async-start(), calls=%async_computation.8 | async-start | bytes 10485760 | tf_op jit(solution)/shard_map/all_gather | solution.py:12
  1275.6 739.1 %all-gather.24.cloned.1.call-start = ((), (), s32[]{:S(2)}) async-start(), calls=%async_computation.7 | async-start | bytes 5242880 | tf_op jit(solution)/shard_map/all_gather | solution.py:12
  1969.5 9.3 copy-start.3
  1969.5 9.3 copy-start.8
  2050.1 119.8 %copy-start.15 = (f32[512,1024]{0,1:T(8,128)S(1)}, f32[512,1024]{0,1:T(8,128)}, u32[]{:S(2)}) copy-start(f32[512,1024]{0,1:T(8,128)} %reduce_sum.59) | copy-start | bytes 6291460
  2170.5 10.7 copy-start.10
  2173.1 8.3 copy-start.16
  2176.7 4.7 copy-start.18
  2201.2 3.6 copy-start.4
  2208.1 6.8 copy-start.12
  2215.0 11.3 copy-start.11
  2215.0 11.3 copy-start.17
  2215.0 11.3 copy-start.25
  2215.0 11.3 copy-start.28
  (8 other events, 15.0 us)
Sparse Core Ops, SparseCore 0:
  9.4 119.7 all-gather.13
  144.4 187.2 reduce-scatter.1
  342.1 637.7 all-gather.15
  981.3 58.2 all-gather.19
  1041.1 34.4 all-gather.17
  1272.5 637.7 all-gather.21
  1911.9 58.2 all-gather.25
  1971.8 34.4 all-gather.23
